TPU v7x, 128 devices: a whole 4x4x4 slice. The times are simulated.
128 devices in a mesh: tm: 8 (over y, core), hash: 16 (over z, x).
Axes of the slice: x: 4, y: 4, z: 4, core: 2. Of those that a mesh axis runs over, the one named last changes fastest.
Arguments:
- fact_blocks: bfloat16 [6144, 128, 128], P(('tm', 'hash'))
- owners: int32 [6144], P(('tm', 'hash')), may hold values from 0 to 15, as said below
- row_counts: int32 [6144], P(('tm', 'hash')), may hold values from 64 to 128
- neighbours: int32 [128, 16, 12], P(('tm', 'hash')), may hold values from 0 to 63
- entities: bfloat16 [1024, 128, 128], P('hash'), may hold values from -6 to 6
- col_gain: float32 [128], replicated, may hold values from 0.1 to 1.9
- w_self: bfloat16 [128, 512], replicated, may hold values from -0.5 to 0.5
- w_nbr: bfloat16 [128, 512], replicated, may hold values from -0.5 to 0.5
- mlp_bias: float32 [512], replicated, may hold values from -3 to 3
- w_mid: bfloat16 [512, 512], replicated, may hold values from -0.25 to 0.25
- w_out: bfloat16 [512, 128], replicated, may hold values from -0.25 to 0.25
Outputs:
- sage_out: bfloat16 [128, 96, 128, 128], P(('tm', 'hash'))
Inputs may be any that keep to these rules, and one draw needn't show every extreme that they name: `owners`: each device sends at most 6 of its blocks to one owner; in every time partition one owner receives exactly 6 blocks from each of the 16 devices, and every owner receives at least one block.
All inputs are finite; a program needn't handle non-finite values.
Results may differ from a plain program's by a relative error of at most 0.011.
Values may be sent and summed in bfloat16 or wider, within the bound.
A program may use at most 128 MiB of HBM per device.

v0:
```python
import jax
import jax.numpy as jnp
from jax import lax
from jax.sharding import PartitionSpec as P

KN = 2


def body(
    fact_blocks,
    owners,
    row_counts,
    neighbours,
    entities,
    col_gain,
    w_self,
    w_nbr,
    mlp_bias,
    w_mid,
    w_out,
):
    holders = lax.axis_size("hash")
    block_count, row_len, feat_width = fact_blocks.shape
    capacity = max(2, 2 * block_count // holders)
    slot_count = holders * capacity
    one_hot = (owners[:, None] == jnp.arange(holders, dtype=jnp.int32)[None, :]).astype(jnp.int32)
    ranking = jnp.sum((jnp.cumsum(one_hot, axis=0) - 1) * one_hot, axis=1)
    target = owners * capacity + ranking
    outgoing = (
        jnp.zeros((slot_count, row_len, feat_width), fact_blocks.dtype).at[target].set(fact_blocks)
    )
    sent_counts = (
        jnp.zeros((slot_count,), jnp.bfloat16).at[target].set(row_counts.astype(jnp.bfloat16))
    )
    received, got_counts = (
        lax.all_to_all(
            outgoing.reshape(holders, capacity, row_len, feat_width),
            "hash",
            split_axis=0,
            concat_axis=0,
            tiled=True,
        ),
        lax.all_to_all(
            sent_counts.reshape(holders, capacity), "hash", split_axis=0, concat_axis=0, tiled=True
        ),
    )
    slot_rows = got_counts.reshape(slot_count, 1).astype(jnp.int32)
    valid = (lax.broadcasted_iota(jnp.int32, (slot_count, row_len), 1) < slot_rows).astype(
        jnp.float32
    )
    values = received.reshape(slot_count, row_len, feat_width).astype(jnp.float32)
    col_sum = jnp.einsum("sr,srd->d", valid, values)
    col_sq = jnp.einsum("sr,srd->d", valid, values * values)
    live = jnp.sum(valid)
    col_sum, col_sq, live = lax.psum((col_sum, col_sq, live), "tm")
    col_mean = col_sum / live
    col_var = col_sq / live - col_mean * col_mean
    normed = ((values - col_mean) * lax.rsqrt(col_var + 1e-05) * col_gain).astype(jnp.bfloat16)
    lists = neighbours[0]
    found = entities[lax.all_to_all(lists, "hash", split_axis=0, concat_axis=0, tiled=True)]
    fetched = lax.all_to_all(found, "hash", split_axis=0, concat_axis=0, tiled=True)
    both = fetched.reshape(holders, capacity, KN, row_len, feat_width).astype(jnp.float32)
    agg = (
        (jnp.sum(both, axis=2) * (1.0 / KN))
        .astype(jnp.bfloat16)
        .reshape(slot_count * row_len, feat_width)
    )
    flat = normed.reshape(slot_count * row_len, feat_width)
    first = (
        jnp.dot(flat, w_self, preferred_element_type=jnp.float32)
        + jnp.dot(agg, w_nbr, preferred_element_type=jnp.float32)
        + mlp_bias
    )
    hidden_one = jnp.maximum(first, 0.0).astype(jnp.bfloat16)
    hidden_two = jnp.maximum(
        jnp.dot(hidden_one, w_mid, preferred_element_type=jnp.float32), 0.0
    ).astype(jnp.bfloat16)
    result = jnp.dot(hidden_two, w_out, preferred_element_type=jnp.float32) * valid.reshape(-1, 1)
    return result.astype(jnp.bfloat16).reshape(1, slot_count, row_len, feat_width)


def solution(mesh):
    return jax.shard_map(
        body,
        mesh=mesh,
        in_specs=(
            P(("tm", "hash"), None, None),
            P(("tm", "hash")),
            P(("tm", "hash")),
            P(("tm", "hash"), None, None),
            P("hash", None, None),
            P(),
            P(),
            P(),
            P(),
            P(),
            P(),
        ),
        out_specs=P(("tm", "hash"), None, None, None),
        check_vma=False,
    )
```

profile of v0, /device:TPU:1, one launch (start us, length us, event | category | flops | bytes accessed | tf_op | source)
XLA Modules:
  0.0 211.5 jit_solution(10846579292963598011)
XLA Ops:
  0.0 0.0 copy-start
  0.0 0.8 convert_element_type.67
  0.8 0.7 fusion.20
  1.5 0.1 reduce_window_sum.11
  1.6 0.8 select_reduce_fusion
  2.4 0.7 compare_select_fusion.1
  3.1 0.9 scatter_custom_fusion.1
  4.0 0.7 all_to_all.27
  4.7 8.4 %all-to-all-start.1 = ((bf16[16,1,6]{2,1,0:T(2,128)(2,1)}), bf16[16,1,6]{2,1,0:T(2,128)(2,1)S(1)}, u32[]{:S(2)}, u32[]{:S(2)}) async-start(bf16[16,1,6]{2,1,0:T(2,128)(2,1)} %all_to_all.27), calls=%async_computation.1 | async-start | bytes 16384 | tf_op jit(solution)/shard_map/all_to_all | solution.py:43
  13.1 1.4 copy.24
  14.5 5.0 %all-to-all-done.1 = bf16[16,1,6]{2,1,0:T(2,128)(2,1)S(1)} async-done(((bf16[16,1,6]{2,1,0:T(2,128)(2,1)}), bf16[16,1,6]{2,1,0:T(2,128)(2,1)S(1)}, u32[]{:S(2)}, u32[]{:S(2)}) %all-to-all-start.1) | async-done | bytes 224 | tf_op jit(solution)/shard_map/all_to_all | solution.py:43
  19.4 3.5 %all-to-all-start.2 = ((s32[16,1,12]{2,1,0:T(1,128)}), s32[16,1,12]{2,1,0:T(1,128)S(1)}, u32[]{:S(2)}, u32[]{:S(2)}) async-start(s32[16,1,12]{2,1,0:T(1,128)} %copy.24), calls=%async_computation.2 | async-start | bytes 16384 | tf_op jit(solution)/shard_map/all_to_all | solution.py:60
  23.0 2.4 %broadcast_in_dim.6 = bf16[96,128,128]{2,1,0:T(8,128)(2,1)} broadcast(bf16[]{:T(256)} %constant.9.clone.1), dimensions={} | broadcast | bytes 3145730 | tf_op jit(solution)/shard_map/broadcast_in_dim | solution.py:30
  25.4 7.6 %scatter_fusion = bf16[96,128,128]{2,1,0:T(8,128)(2,1)} fusion(bf16[96,128,128]{2,1,0:T(8,128)(2,1)} %broadcast_in_dim.6, s32[48]{0:T(128)S(1)} %compare_select_fusion.1, bf16[48,128,128]{2,1,0:T(8,128)(2,1)} %param.11), kind=kCustom, calls=%fused_computation.1 | custom fusion | bytes 4718784 | tf_op jit(solution)/shard_map/scatter | solution.py:30
  33.0 0.0 all-to-all-done.2
  33.0 6.6 %all-to-all-start = ((bf16[16,6,128,128]{3,2,1,0:T(8,128)(2,1)}), bf16[16,6,128,128]{3,2,1,0:T(8,128)(2,1)}, u32[]{:S(2)}, u32[]{:S(2)}) async-start(bf16[16,6,128,128]{3,2,1,0:T(8,128)(2,1)} %bitcast.32), calls=%async_computation | async-start | bytes 6291456 | tf_op jit(solution)/shard_map/all_to_all | solution.py:36
  39.6 0.1 copy.25
  39.7 0.1 copy.26
  39.8 0.1 reshape.99
  39.9 0.0 copy-done
  39.9 8.1 %gather_fusion = bf16[192,128,128]{2,1,0:T(8,128)(2,1)} fusion(bf16[64,128,128]{2,1,0:T(8,128)(2,1)S(1)} %copy-done, s32[1024]{0:T(1024)S(1)} %pad_clamp_fusion), kind=kCustom, calls=%fused_computation | custom fusion | bytes 12583680 | tf_op jit(solution)/shard_map/gather | solution.py:60
  48.0 32.8 %all-to-all-done = bf16[16,6,128,128]{3,2,1,0:T(8,128)(2,1)} async-done(((bf16[16,6,128,128]{3,2,1,0:T(8,128)(2,1)}), bf16[16,6,128,128]{3,2,1,0:T(8,128)(2,1)}, u32[]{:S(2)}, u32[]{:S(2)}) %all-to-all-start) | async-done | bytes 3145760 | tf_op jit(solution)/shard_map/all_to_all | solution.py:36
  80.8 6.1 %all-to-all-start.3 = ((bf16[16,12,128,128]{3,2,1,0:T(8,128)(2,1)}), bf16[16,12,128,128]{3,2,1,0:T(8,128)(2,1)}, u32[]{:S(2)}, u32[]{:S(2)}) async-start(bf16[16,12,128,128]{3,2,1,0:T(8,128)(2,1)} %bitcast.31), calls=%async_computation.3 | async-start | bytes 12582912 | tf_op jit(solution)/shard_map/all_to_all | solution.py:61
  86.8 0.0 copy-start.2
  86.8 0.0 copy-start.3
  86.9 0.1 reshape.94
  87.0 0.7 convert_reduce_fusion.1
  87.7 0.1 convert_bitcast_fusion
  87.8 2.4 %convolution_bitcast_fusion = f32[128]{0:T(128)S(1)} fusion(bf16[96,128,128]{2,1,0:T(8,128)(2,1)} %bitcast.3, pred[96,128,1]{1,0,2:T(32,128)(4,1)S(1)} %get-tuple-element.11), kind=kOutput, calls=%fused_computation.23 | convolution fusion | flops 3145728 | bytes 3158528 | tf_op jit(solution)/shard_map/sr,srd->d/dot_general | solution.py:52
  90.2 2.6 %fusion.14 = f32[128]{0:T(128)S(1)} fusion(bf16[96,128,128]{2,1,0:T(8,128)(2,1)} %bitcast.3, pred[96,128,1]{1,0,2:T(32,128)(4,1)S(1)} %get-tuple-element.11), kind=kOutput, calls=%fused_computation.22 | convolution fusion | flops 6291456 | bytes 3158528 | tf_op jit(solution)/shard_map/sr,srd->d/dot_general | solution.py:53
  92.8 15.6 %all-reduce = (f32[128]{0:T(128)S(1)}, f32[]{:T(128)}, f32[128]{0:T(128)S(1)}) all-reduce(f32[128]{0:T(128)S(1)} %convolution_bitcast_fusion, f32[]{:T(128)} %convert_reduce_fusion.1, f32[128]{0:T(128)S(1)} %fusion.14), channel_id=1, replica_groups=mesh['tm'=8,'hash'=16] {'tm'}, use_global_device_ids=true, to_apply=%region_4.5 | all-reduce | flops 257 | bytes 2056 | tf_op jit(solution)/shard_map/psum | solution.py:55
  108.4 0.7 add_rsqrt_fusion
  109.1 0.0 copy-done.2
  109.1 0.0 copy-done.3
  109.1 12.0 %fusion.9 = f32[12288,512]{1,0:T(8,128)} fusion(bf16[128,512]{1,0:T(8,128)(2,1)S(1)} %copy-done.2, bf16[12288,128]{1,0:T(8,128)(2,1)} %bitcast.13, f32[128]{0:T(128)S(1)} %copy-done.3, f32[128]{0:T(128)S(1)} %get-tuple-element.8, f32[128]{0:T(128)S(1)} %get-tuple-element.9), kind=kOutput, calls=%fused_computation.18 | convolution fusion | flops 1618477056 | bytes 28444160 | tf_op jit(solution)/shard_map/dot_general | solution.py:70
  121.1 55.4 %all-to-all-done.3 = bf16[16,12,128,128]{3,2,1,0:T(8,128)(2,1)} async-done(((bf16[16,12,128,128]{3,2,1,0:T(8,128)(2,1)}), bf16[16,12,128,128]{3,2,1,0:T(8,128)(2,1)}, u32[]{:S(2)}, u32[]{:S(2)}) %all-to-all-start.3) | async-done | bytes 6291488 | tf_op jit(solution)/shard_map/all_to_all | solution.py:61
  176.5 5.4 %convert_reduce_fusion = f32[16,6,128,128]{3,2,1,0:T(8,128)S(1)} fusion(bf16[16,6,2,128,128]{4,3,2,1,0:T(8,128)(2,1)} %bitcast.14), kind=kLoop, calls=%fused_computation.7 | loop fusion | flops 4718592 | bytes 12582912 | tf_op jit(solution)/shard_map/reduce_sum | solution.py:64
  181.9 0.0 copy-start.4
  181.9 0.0 copy-start.5
  181.9 0.0 copy-start.7
  181.9 2.5 %multiply_convert_fusion = bf16[16,6,128,128]{3,2,1,0:T(8,128)(2,1)} fusion(f32[16,6,128,128]{3,2,1,0:T(8,128)S(1)} %convert_reduce_fusion), kind=kLoop, calls=%fused_computation.14 | loop fusion | flops 3145728 | bytes 9437184 | tf_op jit(solution)/shard_map/convert_element_type | solution.py:65
  184.4 0.0 copy-done.4
  184.4 0.0 copy-done.5
  184.4 0.0 copy-done.7
  184.5 19.4 %maximum_convert_fusion = bf16[12288,512]{1,0:T(8,128)(2,1)} fusion(bf16[512,512]{1,0:T(8,128)(2,1)S(1)} %copy-done.4, f32[12288,512]{1,0:T(8,128)} %fusion.9, bf16[12288,128]{1,0:T(8,128)(2,1)} %bitcast.33, bf16[128,512]{1,0:T(8,128)(2,1)S(1)} %copy-done.5, f32[512]{0:T(512)S(1)} %copy-done.7), kind=kOutput, calls=%fused_computation.3 | convolution fusion | flops 8090812416 | bytes 41551872 | tf_op jit(solution)/shard_map/dot_general | solution.py:76
  203.8 0.0 copy-done.6
  203.8 7.7 %fusion = bf16[12288,128]{1,0:T(8,128)(2,1)} fusion(bf16[12288,512]{1,0:T(8,128)(2,1)} %maximum_convert_fusion, bf16[512,128]{1,0:T(8,128)(2,1)S(1)} %copy-done.6, f32[12288]{0:T(1024)S(1)} %get-tuple-element.10), kind=kOutput, calls=%fused_computation.6 | convolution fusion | flops 1613758464 | bytes 15908864 | tf_op jit(solution)/shard_map/dot_general | solution.py:78
  211.5 0.0 copy-done.1
  (5 shorter events, 0.0 us)
Async XLA Ops:
  0.0 39.9 %copy-start = (bf16[64,128,128]{2,1,0:T(8,128)(2,1)S(1)}, bf16[64,128,128]{2,1,0:T(8,128)(2,1)}, u32[]{:S(2)}) copy-start(bf16[64,128,128]{2,1,0:T(8,128)(2,1)} %param.15) | copy-start | bytes 6291460
  4.7 14.8 %all-to-all-start.1 = ((bf16[16,1,6]{2,1,0:T(2,128)(2,1)}), bf16[16,1,6]{2,1,0:T(2,128)(2,1)S(1)}, u32[]{:S(2)}, u32[]{:S(2)}) async-start(bf16[16,1,6]{2,1,0:T(2,128)(2,1)} %all_to_all.27), calls=%async_computation.1 | async-start | bytes 16384 | tf_op jit(solution)/shard_map/all_to_all | solution.py:43
  19.4 13.5 %all-to-all-start.2 = ((s32[16,1,12]{2,1,0:T(1,128)}), s32[16,1,12]{2,1,0:T(1,128)S(1)}, u32[]{:S(2)}, u32[]{:S(2)}) async-start(s32[16,1,12]{2,1,0:T(1,128)} %copy.24), calls=%async_computation.2 | async-start | bytes 16384 | tf_op jit(solution)/shard_map/all_to_all | solution.py:60
  33.0 47.8 %all-to-all-start = ((bf16[16,6,128,128]{3,2,1,0:T(8,128)(2,1)}), bf16[16,6,128,128]{3,2,1,0:T(8,128)(2,1)}, u32[]{:S(2)}, u32[]{:S(2)}) async-start(bf16[16,6,128,128]{3,2,1,0:T(8,128)(2,1)} %bitcast.32), calls=%async_computation | async-start | bytes 6291456 | tf_op jit(solution)/shard_map/all_to_all | solution.py:36
  80.8 95.7 %all-to-all-start.3 = ((bf16[16,12,128,128]{3,2,1,0:T(8,128)(2,1)}), bf16[16,12,128,128]{3,2,1,0:T(8,128)(2,1)}, u32[]{:S(2)}, u32[]{:S(2)}) async-start(bf16[16,12,128,128]{3,2,1,0:T(8,128)(2,1)} %bitcast.31), calls=%async_computation.3 | async-start | bytes 12582912 | tf_op jit(solution)/shard_map/all_to_all | solution.py:61
  86.8 22.2 %copy-start.2 = (bf16[128,512]{1,0:T(8,128)(2,1)S(1)}, bf16[128,512]{1,0:T(8,128)(2,1)}, u32[]{:S(2)}) copy-start(bf16[128,512]{1,0:T(8,128)(2,1)} %param.17) | copy-start | bytes 393220
  86.8 22.2 %copy-start.3 = (f32[128]{0:T(128)S(1)}, f32[128]{0:T(128)}, u32[]{:S(2)}) copy-start(f32[128]{0:T(128)} %param.16) | copy-start | bytes 1540
  181.9 2.5 %copy-start.4 = (bf16[512,512]{1,0:T(8,128)(2,1)S(1)}, bf16[512,512]{1,0:T(8,128)(2,1)}, u32[]{:S(2)}) copy-start(bf16[512,512]{1,0:T(8,128)(2,1)} %param.20) | copy-start | bytes 1572868
  181.9 2.5 %copy-start.5 = (bf16[128,512]{1,0:T(8,128)(2,1)S(1)}, bf16[128,512]{1,0:T(8,128)(2,1)}, u32[]{:S(2)}) copy-start(bf16[128,512]{1,0:T(8,128)(2,1)} %param.18) | copy-start | bytes 393220
  181.9 2.5 %copy-start.7 = (f32[512]{0:T(512)S(1)}, f32[512]{0:T(512)}, u32[]{:S(2)}) copy-start(f32[512]{0:T(512)} %param.19) | copy-start | bytes 6148
  184.4 19.4 %copy-start.6 = (bf16[512,128]{1,0:T(8,128)(2,1)S(1)}, bf16[512,128]{1,0:T(8,128)(2,1)}, u32[]{:S(2)}) copy-start(bf16[512,128]{1,0:T(8,128)(2,1)} %param.21) | copy-start | bytes 393220
  203.8 7.7 %copy-start.1 = (bf16[64,128,128]{2,1,0:T(8,128)(2,1)S(1)}, bf16[64,128,128]{2,1,0:T(8,128)(2,1)}, u32[]{:S(2)}) copy-start(bf16[64,128,128]{2,1,0:T(8,128)(2,1)} %param.15) | copy-start | bytes 6291460
where the time goes:
time: 214 us; the launch traced here: 212 us
  waiting for transfers between devices  93.1 us (44%)
  matrix products  44.2 us (21%)
  starting transfers between devices  24.6 us (11%)
  local copies, waits for them, and re-layouts  21.4 us (10%)
  blocking collectives  15.6 us (7%)
  other arithmetic  12.5 us (6%)
    all_to_all x1, waiting for transfers between devices, body(): lax.all_to_all(found, 'hash', split_axis=0, concat_axis=0, tiled=True)  55.4 us
    all_to_all x1, waiting for transfers between devices, body(): lax.all_to_all(outgoing.reshape(holders, capacity, row_len, feat_width),...  32.8 us
    dot_general x1, matrix products, body(): jnp.dot(hidden_one, w_mid, preferred_element_type=jnp.float32)  19.4 us
    psum x1, blocking collectives, body(): col_sum, col_sq, live = lax.psum((col_sum, col_sq, live), 'tm')  15.6 us
    dot_general x1, matrix products, body(): jnp.dot(flat, w_self, preferred_element_type=jnp.float32)  12 us
    all_to_all x1, starting transfers between devices, body(): lax.all_to_all(sent_counts.reshape(holders, capacity), 'hash', split_axis...  8.43 us
    gather x1, local copies, waits for them, and re-layouts, body(): entities[lax.all_to_all(lists, 'hash', split_axis=0, concat_axis=0, tiled...  8.07 us
    dot_general x1, matrix products, body(): jnp.dot(hidden_two, w_out, preferred_element_type=jnp.float32)  7.7 us
  transfers between devices with their start and end apart: 4, of which 3 were waited for; matrix products, arithmetic and copies ran while one was open for 18% of the time, Pallas kernels for 0%

commit v1 on v0

v1 whole, which is shorter than its diff:
```python
import functools

import jax
import jax.numpy as jnp
from jax import lax
from jax.experimental import pallas as pl
from jax.experimental.pallas import tpu as pltpu
from jax.sharding import PartitionSpec as P

MESH = pl.DeviceIdType.MESH
HOLD = 16
TM = 8
CAP = 6
B = 48
R = 128
D = 128
HID = 512
EPS = 1e-05
CHUNKS = 4
F32 = jnp.float32
BF16 = jnp.bfloat16


def peer(s, dz, dx):
    return lax.rem(lax.div(s, 4) + dz, 4) * 4 + lax.rem(lax.rem(s, 4) + dx, 4)


def kernel(
    fact_hbm, own_v, cnt_v, cnt_s, nb_v, ent_hbm, gain_v, wself_hbm, wnbr_hbm, bias_v, wmid_hbm, wout_hbm,
    o_ref,
    facts, ent, w1, wmid, wout, bs, bq, st, r1, r2, fin, nbs, rnb, tab_v, nbt_v, tab_s, nb_s, mean_v, scale_v,
    in1, send, lsem, s1, q1, s2, q2, s3, q3, sn, qn, ss, qs,
):
    t = lax.axis_index("tm")
    s = lax.axis_index("hash")

    bar = pltpu.get_barrier_semaphore()
    for i in range(1, TM):
        pl.semaphore_signal(bar, inc=1, device_id={"tm": lax.rem(t + i, TM)}, device_id_type=MESH)
    for d in range(1, HOLD):
        pl.semaphore_signal(bar, inc=1, device_id={"hash": peer(s, d // 4, d % 4)}, device_id_type=MESH)

    per = B // CHUNKS
    loads = [
        pltpu.make_async_copy(fact_hbm.at[pl.ds(k * per, per)], facts.at[pl.ds(k * per, per)], lsem.at[k])
        for k in range(CHUNKS)
    ]
    rest = [
        pltpu.make_async_copy(wself_hbm, w1.at[pl.ds(0, D)], lsem.at[CHUNKS]),
        pltpu.make_async_copy(wnbr_hbm, w1.at[pl.ds(D, D)], lsem.at[CHUNKS + 1]),
        pltpu.make_async_copy(wmid_hbm, wmid, lsem.at[CHUNKS + 2]),
        pltpu.make_async_copy(wout_hbm, wout, lsem.at[CHUNKS + 3]),
        pltpu.make_async_copy(ent_hbm, ent, lsem.at[CHUNKS + 4]),
    ]
    for cp in loads + rest:
        cp.start()

    hot = (lax.broadcasted_iota(jnp.int32, (HOLD, B), 0) == own_v[...]).astype(F32)
    upper = (
        lax.broadcasted_iota(jnp.int32, (B, B), 0) <= lax.broadcasted_iota(jnp.int32, (B, B), 1)
    ).astype(BF16)
    order = jnp.dot(hot.astype(BF16), upper, preferred_element_type=F32)
    cnt = cnt_v[...].astype(F32)
    blk = lax.broadcasted_iota(jnp.int32, (HOLD, B), 1).astype(F32)
    lane = lax.broadcasted_iota(jnp.int32, (HOLD, 128), 1)
    tab = jnp.zeros((HOLD, 128), F32)
    for c in range(CAP):
        sel = jnp.where(order == float(c + 1), hot, 0.0)
        tab = jnp.where(lane == c, jnp.sum(sel * blk, axis=1, keepdims=True), tab)
        tab = jnp.where(lane == 8 + c, jnp.sum(sel * cnt, axis=1, keepdims=True), tab)
    tab_v[...] = tab.astype(jnp.int32)
    tab_copy = pltpu.make_async_copy(tab_v, tab_s, lsem.at[CHUNKS + 5])
    tab_copy.start()

    nbs[...] = jnp.zeros_like(nbs)
    nbt_v[...] = jnp.zeros_like(nbt_v)
    for q in range(2 * CAP):
        nbt_v[q : q + 1, 0:HOLD] = nb_v[q]
    lists = nbt_v[...].T
    for j in range(HOLD):
        nbs[j, 0:1, 0:HOLD] = lists[j : j + 1, :]

    row = lax.broadcasted_iota(jnp.int32, (R, D), 0)
    for k in range(CHUNKS):
        loads[k].wait()

        def stat(i, carry):
            for j in range(2):
                b = k * per + i * 2 + j
                x = jnp.where(row < cnt_s[b], facts[b].astype(F32), 0.0)
                bs[pl.ds(b, 1), :] = jnp.sum(x, axis=0, keepdims=True)
                bq[pl.ds(b, 1), :] = jnp.sum(x * x, axis=0, keepdims=True)
            return carry

        lax.fori_loop(0, per // 2, stat, 0)
    sums = jnp.dot(hot, bs[...], preferred_element_type=F32, precision=lax.Precision.HIGHEST)
    squares = jnp.dot(hot, bq[...], preferred_element_type=F32, precision=lax.Precision.HIGHEST)
    live = jnp.broadcast_to(jnp.sum(hot * cnt, axis=1, keepdims=True), (HOLD, 128))
    st[...] = jnp.zeros_like(st)
    for h in range(HOLD):
        base = 3 * (h % 2)
        st[h // 2, base : base + 1, :] = sums[h : h + 1, :]
        st[h // 2, base + 1 : base + 2, :] = squares[h : h + 1, :]
        st[h // 2, base + 2 : base + 3, :] = live[h : h + 1, :]

    pl.semaphore_wait(bar, TM - 1 + HOLD - 1)

    first = []
    for i in range(1, TM):
        p = lax.rem(t + i, TM)
        first.append(
            pltpu.make_async_remote_copy(
                src_ref=st.at[p], dst_ref=r1.at[t], send_sem=s1.at[i], recv_sem=q1.at[i],
                device_id={"tm": p}, device_id_type=MESH,
            )
        )
        first[-1].start()
    asks = []
    for d in range(1, HOLD):
        p = peer(s, d // 4, d % 4)
        asks.append(
            pltpu.make_async_remote_copy(
                src_ref=nbs.at[p], dst_ref=rnb.at[s], send_sem=sn.at[d], recv_sem=qn.at[d],
                device_id={"hash": p}, device_id_type=MESH,
            )
        )
        asks[-1].start()
    rnb[s] = nbs[s]
    r1[t] = st[t]
    for cp in first:
        cp.wait_recv()
    r2[s] = jnp.sum(r1[...], axis=0)
    second = []
    for d in range(1, HOLD):
        p = peer(s, d // 4, d % 4)
        second.append(
            pltpu.make_async_remote_copy(
                src_ref=r2.at[s], dst_ref=r2.at[s], send_sem=s2.at[d], recv_sem=q2.at[d],
                device_id={"hash": p}, device_id_type=MESH,
            )
        )
        second[-1].start()
    for cp in asks:
        cp.wait_recv()
    for h in range(HOLD):
        nbt_v[h : h + 1, :] = rnb[h, 0:1, :]
    nb_copy = pltpu.make_async_copy(nbt_v, nb_s, lsem.at[CHUNKS + 6])
    nb_copy.start()
    for cp in rest:
        cp.wait()
    for cp in second:
        cp.wait_recv()
    fin[t] = jnp.sum(r2[...], axis=0)
    third = []
    for i in range(1, TM):
        p = lax.rem(t + i, TM)
        third.append(
            pltpu.make_async_remote_copy(
                src_ref=fin.at[t], dst_ref=fin.at[t], send_sem=s3.at[i], recv_sem=q3.at[i],
                device_id={"tm": p}, device_id_type=MESH,
            )
        )
        third[-1].start()
    tab_copy.wait()
    nb_copy.wait()
    for cp in third:
        cp.wait_recv()
    for h in range(HOLD):
        base = 3 * (h % 2)
        n = fin[h // 2, base + 2 : base + 3, :]
        mean = fin[h // 2, base : base + 1, :] / n
        var = fin[h // 2, base + 1 : base + 2, :] / n - mean * mean
        mean_v[h : h + 1, :] = mean
        scale_v[h : h + 1, :] = lax.rsqrt(var + EPS) * gain_v[...]

    def copy_of(dz, dx, c):
        k = (dz * 4 + dx) * CAP + c
        return pltpu.make_async_remote_copy(
            src_ref=send.at[k], dst_ref=o_ref.at[s * CAP + c], send_sem=ss.at[k], recv_sem=qs.at[k],
            device_id={"hash": peer(s, dz, dx)}, device_id_type=MESH,
        )

    def step(n, carry):
        c, dz = lax.div(n, 4), lax.rem(n, 4)
        for dx in range(4):
            p = peer(s, dz, dx)
            x = facts[jnp.clip(tab_s[p, c], 0, B - 1)].astype(F32)
            x = (x - mean_v[pl.ds(p, 1), :]) * scale_v[pl.ds(p, 1), :]
            in1[dx * R : (dx + 1) * R, 0:D] = x.astype(BF16)
            e = ent[nb_s[p, 2 * c]].astype(F32) + ent[nb_s[p, 2 * c + 1]].astype(F32)
            in1[dx * R : (dx + 1) * R, D : 2 * D] = (e * 0.5).astype(BF16)
        h1 = jnp.dot(in1[...], w1[...], preferred_element_type=F32) + bias_v[...]
        h1 = jnp.maximum(h1, 0.0).astype(BF16)
        h2 = jnp.dot(h1, wmid[...], preferred_element_type=F32)
        h2 = jnp.maximum(h2, 0.0).astype(BF16)
        out = jnp.dot(h2, wout[...], preferred_element_type=F32)
        for dx in range(4):
            p = peer(s, dz, dx)
            y = jnp.where(row < tab_s[p, 8 + c], out[dx * R : (dx + 1) * R, :], 0.0).astype(BF16)
            send[(dz * 4 + dx) * CAP + c] = y
            if dx:
                copy_of(dz, dx, c).start()
            else:

                @pl.when(dz > 0)
                def _():
                    copy_of(dz, 0, c).start()

                @pl.when(dz == 0)
                def _():
                    o_ref[s * CAP + c] = y

        return carry

    lax.fori_loop(0, 4 * CAP, step, 0)

    for cp in first + asks + second + third:
        cp.wait_send()

    def finish(k, carry):
        d, c = lax.div(k, CAP) + 1, lax.rem(k, CAP)
        copy_of(lax.div(d, 4), lax.rem(d, 4), c).wait()
        return carry

    lax.fori_loop(0, (HOLD - 1) * CAP, finish, 0)


def body(fact_blocks, owners, row_counts, neighbours, entities, col_gain, w_self, w_nbr, mlp_bias, w_mid, w_out):
    vmem = pl.BlockSpec(memory_space=pltpu.VMEM)
    smem = pl.BlockSpec(memory_space=pltpu.SMEM)
    hbm = pl.BlockSpec(memory_space=pl.ANY)
    dma = pltpu.SemaphoreType.DMA
    out = pl.pallas_call(
        kernel,
        out_shape=jax.ShapeDtypeStruct((HOLD * CAP, R, D), BF16),
        in_specs=[hbm, vmem, vmem, smem, vmem, hbm, vmem, hbm, hbm, vmem, hbm, hbm],
        out_specs=vmem,
        scratch_shapes=[
            pltpu.VMEM((B, R, D), BF16),
            pltpu.VMEM((64, R, D), BF16),
            pltpu.VMEM((2 * D, HID), BF16),
            pltpu.VMEM((HID, HID), BF16),
            pltpu.VMEM((HID, D), BF16),
            pltpu.VMEM((B, D), F32),
            pltpu.VMEM((B, D), F32),
            pltpu.VMEM((TM, 8, 128), F32),
            pltpu.VMEM((TM, 8, 128), F32),
            pltpu.VMEM((HOLD, 8, 128), F32),
            pltpu.VMEM((TM, 8, 128), F32),
            pltpu.VMEM((HOLD, 8, 128), jnp.int32),
            pltpu.VMEM((HOLD, 8, 128), jnp.int32),
            pltpu.VMEM((HOLD, 128), jnp.int32),
            pltpu.VMEM((HOLD, 128), jnp.int32),
            pltpu.SMEM((HOLD, 128), jnp.int32),
            pltpu.SMEM((HOLD, 128), jnp.int32),
            pltpu.VMEM((HOLD, D), F32),
            pltpu.VMEM((HOLD, D), F32),
            pltpu.VMEM((4 * R, 2 * D), BF16),
            pltpu.VMEM((HOLD * CAP, R, D), BF16),
            dma((CHUNKS + 7,)),
            dma((TM,)), dma((TM,)),
            dma((HOLD,)), dma((HOLD,)),
            dma((TM,)), dma((TM,)),
            dma((HOLD,)), dma((HOLD,)),
            dma((HOLD * CAP,)), dma((HOLD * CAP,)),
        ],
        compiler_params=pltpu.CompilerParams(
            collective_id=0, has_side_effects=True, vmem_limit_bytes=60 << 20
        ),
        cost_estimate=pl.CostEstimate(flops=12 * 10**9, bytes_accessed=10 * 2**20, transcendentals=0),
    )(
        fact_blocks,
        owners.reshape(1, B),
        row_counts.reshape(1, B),
        row_counts,
        neighbours.transpose(2, 0, 1),
        entities,
        col_gain.reshape(1, D),
        w_self,
        w_nbr,
        mlp_bias.reshape(1, HID),
        w_mid,
        w_out,
    )
    return out[None]


def solution(mesh):
    return jax.shard_map(
        body,
        mesh=mesh,
        in_specs=(
            P(("tm", "hash"), None, None),
            P(("tm", "hash")),
            P(("tm", "hash")),
            P(("tm", "hash"), None, None),
            P("hash", None, None),
            P(),
            P(),
            P(),
            P(),
            P(),
            P(),
        ),
        out_specs=P(("tm", "hash"), None, None, None),
        check_vma=False,
    )
```

time: 214 us -> 68.1 us (0.32); the launches traced: 212 us -> 68 us
  waiting for transfers between devices: 93.1 us -> 0 us
  Pallas kernels: 0 us -> 64 us
  matrix products: 44.2 us -> 0 us
  starting transfers between devices: 24.6 us -> 0 us
  local copies, waits for them, and re-layouts: 21.4 us -> 3.97 us
  blocking collectives: 15.6 us -> 0 us
  other arithmetic: 12.5 us -> 0 us
    all_to_all x4 -> x0, waiting for transfers between devices: 93.1 us -> none  [the longest x1 55.4 us: body(): lax.all_to_all(found, 'hash', split_axis=0, concat_axis=0, tiled=True)]
    pallas_call x0 -> x1, Pallas kernels: none -> 64 us  [body(): pl.pallas_call(kernel, out_shape=jax.ShapeDtypeStruct((HOLD * CAP, R, D),...]
    dot_general x5 -> x0, matrix products: 44.2 us -> none  [the longest x1 19.4 us: body(): jnp.dot(hidden_one, w_mid, preferred_element_type=jnp.float32)]
    all_to_all x4 -> x0, starting transfers between devices: 24.6 us -> none  [the longest x1 8.43 us: body(): lax.all_to_all(sent_counts.reshape(holders, capacity), 'hash', split_axis...]
    psum x1 -> x0, blocking collectives: 15.6 us -> none  [body(): col_sum, col_sq, live = lax.psum((col_sum, col_sq, live), 'tm')]
    scatter x2 -> x0, local copies, waits for them, and re-layouts: 8.43 us -> none  [the longest x1 7.58 us: body(): jnp.zeros((slot_count, row_len, feat_width), fact_blocks.dtype).at[target]]
    gather x1 -> x0, local copies, waits for them, and re-layouts: 8.07 us -> none  [body(): entities[lax.all_to_all(lists, 'hash', split_axis=0, concat_axis=0, tiled...]
    reduce_sum x3 -> x0, other arithmetic: 6.91 us -> none  [the longest x1 5.39 us: body(): jnp.sum(both, axis=2) * (1.0 / KN)]
  transfers between devices with their start and end apart: 4 -> 0, of which waited for: 3 -> 0; matrix products, arithmetic and copies ran while one was open for 18% -> 0% of each run, Pallas kernels for 0% -> 0%
where the time goes in v1:
time: 68.1 us; the launch traced here: 68 us
  Pallas kernels  64 us (94%)
  local copies, waits for them, and re-layouts  3.97 us (6%)
    pallas_call x1, Pallas kernels, body(): pl.pallas_call(kernel, out_shape=jax.ShapeDtypeStruct((HOLD * CAP, R, D),...  64 us
    unnamed x1, local copies, waits for them, and re-layouts  3.97 us

profile of v1, /device:TPU:1, one launch (start us, length us, event | category | flops | bytes accessed | tf_op | source)
XLA Modules:
  0.0 68.0 jit_solution(14341595634967122778)
XLA Ops:
  0.0 64.0 %shard_map.109 = bf16[96,128,128]{2,1,0:T(8,128)(2,1)} custom-call(bf16[48,128,128]{2,1,0:T(8,128)(2,1)} %fact_hbm.1, s32[1,48]{1,0:T(1,128)} %bitcast.9, s32[1,48]{1,0:T(1,128)} %bitcast.10, s32[48]{0:T(128)} %cnt_s.1, s32[12,1,16]{2,1,0:T(1,128)} %bitcast.7, bf16[64,128,128]{2,1,0:T(8,128)(2,1)} %ent_hbm.1, f32[1,128]{1,0:T(1,128)} %bitcast.11, ...), custom_call_target="tpu_custom_call" | custom-call | flops 12000000000 | bytes 10485760 | tf_op jit(solution)/shard_map/pallas_call | solution.py:233
  64.0 4.0 %copy.13 = bf16[1,96,128,128]{3,2,1,0:T(8,128)(2,1)} copy(bf16[1,96,128,128]{3,2,1,0:T(8,128)(2,1)} %bitcast.6) | data formatting | bytes 6291456

commit v2 on v1

--- a/solution.py
+++ b/solution.py
@@ -28,8 +28,8 @@
 def kernel(
     fact_hbm, own_v, cnt_v, cnt_s, nb_v, ent_hbm, gain_v, wself_hbm, wnbr_hbm, bias_v, wmid_hbm, wout_hbm,
     o_ref,
-    facts, ent, w1, wmid, wout, bs, bq, st, r1, r2, fin, nbs, rnb, tab_v, nbt_v, tab_s, nb_s, mean_v, scale_v,
-    in1, send, lsem, s1, q1, s2, q2, s3, q3, sn, qn, ss, qs,
+    facts, ent, w1, wmid, wout, bs, bq, st, r1, r2, fin, nbs, rnb, wide, tab_v, nbt_v, tab_s, nb_s, mean_v, scale_v,
+    in1, send, xs, ags, ex, ea, lsem, s1, q1, s2, q2, s3, q3, sn, qn, sx, qx, sa, qa, ss, qs,
 ):
     t = lax.axis_index("tm")
     s = lax.axis_index("hash")
@@ -67,18 +67,17 @@
     for c in range(CAP):
         sel = jnp.where(order == float(c + 1), hot, 0.0)
         tab = jnp.where(lane == c, jnp.sum(sel * blk, axis=1, keepdims=True), tab)
-        tab = jnp.where(lane == 8 + c, jnp.sum(sel * cnt, axis=1, keepdims=True), tab)
+        tab = jnp.where(lane == 16 + c, jnp.sum(sel * cnt, axis=1, keepdims=True), tab)
     tab_v[...] = tab.astype(jnp.int32)
     tab_copy = pltpu.make_async_copy(tab_v, tab_s, lsem.at[CHUNKS + 5])
     tab_copy.start()
 
-    nbs[...] = jnp.zeros_like(nbs)
-    nbt_v[...] = jnp.zeros_like(nbt_v)
+    wide[...] = jnp.zeros_like(wide)
     for q in range(2 * CAP):
-        nbt_v[q : q + 1, 0:HOLD] = nb_v[q]
-    lists = nbt_v[...].T
+        wide[q : q + 1, 0:HOLD] = nb_v[q]
+    note = jnp.where(lane < 16, wide[...].T[0:HOLD, :], tab_v[...])
     for j in range(HOLD):
-        nbs[j, 0:1, 0:HOLD] = lists[j : j + 1, :]
+        nbs[j] = note[j : j + 1, :]
 
     row = lax.broadcasted_iota(jnp.int32, (R, D), 0)
     for k in range(CHUNKS):
@@ -103,6 +102,15 @@
         st[h // 2, base + 1 : base + 2, :] = squares[h : h + 1, :]
         st[h // 2, base + 2 : base + 3, :] = live[h : h + 1, :]
 
+    tab_copy.wait()
+    for d in range(HOLD):
+        p = peer(s, d // 4, d % 4)
+        x = facts[jnp.clip(tab_s[p, CAP - 1], 0, B - 1)]
+        if d:
+            xs[p] = x
+        else:
+            ex[s] = x
+
     pl.semaphore_wait(bar, TM - 1 + HOLD - 1)
 
     first = []
@@ -125,6 +133,16 @@
             )
         )
         asks[-1].start()
+    early = []
+    for d in range(1, HOLD):
+        p = peer(s, d // 4, d % 4)
+        early.append(
+            pltpu.make_async_remote_copy(
+                src_ref=xs.at[p], dst_ref=ex.at[s], send_sem=sx.at[d], recv_sem=qx.at[d],
+                device_id={"hash": p}, device_id_type=MESH,
+            )
+        )
+        early[-1].start()
     rnb[s] = nbs[s]
     r1[t] = st[t]
     for cp in first:
@@ -143,11 +161,30 @@
     for cp in asks:
         cp.wait_recv()
     for h in range(HOLD):
-        nbt_v[h : h + 1, :] = rnb[h, 0:1, :]
+        nbt_v[h : h + 1, :] = rnb[h]
     nb_copy = pltpu.make_async_copy(nbt_v, nb_s, lsem.at[CHUNKS + 6])
     nb_copy.start()
     for cp in rest:
         cp.wait()
+    nb_copy.wait()
+
+    def agg_of(p, c):
+        e = ent[nb_s[p, 2 * c]].astype(F32) + ent[nb_s[p, 2 * c + 1]].astype(F32)
+        return (e * 0.5).astype(BF16)
+
+    for d in range(HOLD):
+        p = peer(s, d // 4, d % 4)
+        if d:
+            ags[p] = agg_of(p, CAP - 1)
+            early.append(
+                pltpu.make_async_remote_copy(
+                    src_ref=ags.at[p], dst_ref=ea.at[s], send_sem=sa.at[d], recv_sem=qa.at[d],
+                    device_id={"hash": p}, device_id_type=MESH,
+                )
+            )
+            early[-1].start()
+        else:
+            ea[s] = agg_of(p, CAP - 1)
     for cp in second:
         cp.wait_recv()
     fin[t] = jnp.sum(r2[...], axis=0)
@@ -161,8 +198,6 @@
             )
         )
         third[-1].start()
-    tab_copy.wait()
-    nb_copy.wait()
     for cp in third:
         cp.wait_recv()
     for h in range(HOLD):
@@ -180,24 +215,31 @@
             device_id={"hash": peer(s, dz, dx)}, device_id_type=MESH,
         )
 
+    def own_copy(c):
+        return pltpu.make_async_copy(send.at[c], o_ref.at[s * CAP + c], ss.at[c])
+
+    def norm_of(x, p):
+        x = (x.astype(F32) - mean_v[pl.ds(p, 1), :]) * scale_v[pl.ds(p, 1), :]
+        return x.astype(BF16)
+
+    def layers():
+        h1 = jnp.dot(in1[...], w1[...], preferred_element_type=F32) + bias_v[...]
+        h1 = jnp.maximum(h1, 0.0).astype(BF16)
+        h2 = jnp.dot(h1, wmid[...], preferred_element_type=F32)
+        h2 = jnp.maximum(h2, 0.0).astype(BF16)
+        return jnp.dot(h2, wout[...], preferred_element_type=F32)
+
     def step(n, carry):
         c, dz = lax.div(n, 4), lax.rem(n, 4)
         for dx in range(4):
             p = peer(s, dz, dx)
-            x = facts[jnp.clip(tab_s[p, c], 0, B - 1)].astype(F32)
-            x = (x - mean_v[pl.ds(p, 1), :]) * scale_v[pl.ds(p, 1), :]
-            in1[dx * R : (dx + 1) * R, 0:D] = x.astype(BF16)
-            e = ent[nb_s[p, 2 * c]].astype(F32) + ent[nb_s[p, 2 * c + 1]].astype(F32)
-            in1[dx * R : (dx + 1) * R, D : 2 * D] = (e * 0.5).astype(BF16)
-        h1 = jnp.dot(in1[...], w1[...], preferred_element_type=F32) + bias_v[...]
-        h1 = jnp.maximum(h1, 0.0).astype(BF16)
-        h2 = jnp.dot(h1, wmid[...], preferred_element_type=F32)
-        h2 = jnp.maximum(h2, 0.0).astype(BF16)
-        out = jnp.dot(h2, wout[...], preferred_element_type=F32)
+            in1[dx * R : (dx + 1) * R, 0:D] = norm_of(facts[jnp.clip(tab_s[p, c], 0, B - 1)], p)
+            in1[dx * R : (dx + 1) * R, D : 2 * D] = agg_of(p, c)
+        out = layers()
         for dx in range(4):
             p = peer(s, dz, dx)
-            y = jnp.where(row < tab_s[p, 8 + c], out[dx * R : (dx + 1) * R, :], 0.0).astype(BF16)
-            send[(dz * 4 + dx) * CAP + c] = y
+            y = jnp.where(row < tab_s[p, 16 + c], out[dx * R : (dx + 1) * R, :], 0.0)
+            send[(dz * 4 + dx) * CAP + c] = y.astype(BF16)
             if dx:
                 copy_of(dz, dx, c).start()
             else:
@@ -208,21 +250,46 @@
 
                 @pl.when(dz == 0)
                 def _():
-                    o_ref[s * CAP + c] = y
+                    own_copy(c).start()
 
         return carry
 
-    lax.fori_loop(0, 4 * CAP, step, 0)
-
-    for cp in first + asks + second + third:
+    lax.fori_loop(0, 4 * (CAP - 1), step, 0)
+
+    for cp in early:
+        cp.wait_recv()
+
+    def late_copy(k):
+        return pltpu.make_async_copy(ea.at[k], o_ref.at[k * CAP + CAP - 1], ss.at[k * CAP + CAP - 1])
+
+    def late(n, carry):
+        for i in range(4):
+            k = n * 4 + i
+            in1[i * R : (i + 1) * R, 0:D] = norm_of(ex[k], s)
+            in1[i * R : (i + 1) * R, D : 2 * D] = ea[k]
+        out = layers()
+        for i in range(4):
+            k = n * 4 + i
+            y = jnp.where(row < nb_s[k, 16 + CAP - 1], out[i * R : (i + 1) * R, :], 0.0)
+            ea[k] = y.astype(BF16)
+            late_copy(k).start()
+        return carry
+
+    lax.fori_loop(0, HOLD // 4, late, 0)
+
+    for cp in first + asks + second + third + early:
         cp.wait_send()
+    for c in range(CAP - 1):
+        own_copy(c).wait()
+    for k in range(HOLD):
+        late_copy(k).wait()
 
     def finish(k, carry):
-        d, c = lax.div(k, CAP) + 1, lax.rem(k, CAP)
+        d, c = lax.div(k, CAP - 1) + 1, lax.rem(k, CAP - 1)
         copy_of(lax.div(d, 4), lax.rem(d, 4), c).wait()
         return carry
 
-    lax.fori_loop(0, (HOLD - 1) * CAP, finish, 0)
+    lax.fori_loop(0, (HOLD - 1) * (CAP - 1), finish, 0)
 
 
 def body(fact_blocks, owners, row_counts, neighbours, entities, col_gain, w_self, w_nbr, mlp_bias, w_mid, w_out):
@@ -234,7 +301,7 @@
         kernel,
         out_shape=jax.ShapeDtypeStruct((HOLD * CAP, R, D), BF16),
         in_specs=[hbm, vmem, vmem, smem, vmem, hbm, vmem, hbm, hbm, vmem, hbm, hbm],
-        out_specs=vmem,
+        out_specs=hbm,
         scratch_shapes=[
             pltpu.VMEM((B, R, D), BF16),
             pltpu.VMEM((64, R, D), BF16),
@@ -247,8 +314,9 @@
             pltpu.VMEM((TM, 8, 128), F32),
             pltpu.VMEM((HOLD, 8, 128), F32),
             pltpu.VMEM((TM, 8, 128), F32),
-            pltpu.VMEM((HOLD, 8, 128), jnp.int32),
-            pltpu.VMEM((HOLD, 8, 128), jnp.int32),
+            pltpu.VMEM((HOLD, 1, 128), jnp.int32),
+            pltpu.VMEM((HOLD, 1, 128), jnp.int32),
+            pltpu.VMEM((128, 128), jnp.int32),
             pltpu.VMEM((HOLD, 128), jnp.int32),
             pltpu.VMEM((HOLD, 128), jnp.int32),
             pltpu.SMEM((HOLD, 128), jnp.int32),
@@ -257,10 +325,16 @@
             pltpu.VMEM((HOLD, D), F32),
             pltpu.VMEM((4 * R, 2 * D), BF16),
             pltpu.VMEM((HOLD * CAP, R, D), BF16),
+            pltpu.VMEM((HOLD, R, D), BF16),
+            pltpu.VMEM((HOLD, R, D), BF16),
+            pltpu.VMEM((HOLD, R, D), BF16),
+            pltpu.VMEM((HOLD, R, D), BF16),
             dma((CHUNKS + 7,)),
             dma((TM,)), dma((TM,)),
             dma((HOLD,)), dma((HOLD,)),
             dma((TM,)), dma((TM,)),
+            dma((HOLD,)), dma((HOLD,)),
+            dma((HOLD,)), dma((HOLD,)),
             dma((HOLD,)), dma((HOLD,)),
             dma((HOLD * CAP,)), dma((HOLD * CAP,)),
         ],

time: 68.1 us -> 63.6 us (0.934)
  Pallas kernels: 64 us -> 59.5 us
    pallas_call x1, Pallas kernels: 64 us -> 59.5 us  [body(): pl.pallas_call(kernel, out_shape=jax.ShapeDtypeStruct((HOLD * CAP, R, D),...]
where the time goes in v2:
time: 63.6 us; the launch traced here: 63.4 us
  Pallas kernels  59.5 us (94%)
  local copies, waits for them, and re-layouts  3.97 us (6%)
    pallas_call x1, Pallas kernels, body(): pl.pallas_call(kernel, out_shape=jax.ShapeDtypeStruct((HOLD * CAP, R, D),...  59.5 us
    unnamed x1, local copies, waits for them, and re-layouts  3.97 us

profile of v2, /device:TPU:1, one launch (start us, length us, event | category | flops | bytes accessed | tf_op | source)
XLA Modules:
  0.0 63.4 jit_solution(11256561244114495602)
XLA Ops:
  0.0 59.5 %shard_map.109 = bf16[96,128,128]{2,1,0:T(8,128)(2,1)} custom-call(bf16[48,128,128]{2,1,0:T(8,128)(2,1)} %fact_hbm.1, s32[1,48]{1,0:T(1,128)} %bitcast.9, s32[1,48]{1,0:T(1,128)} %bitcast.10, s32[48]{0:T(128)} %cnt_s.1, s32[12,1,16]{2,1,0:T(1,128)} %bitcast.7, bf16[64,128,128]{2,1,0:T(8,128)(2,1)} %ent_hbm.1, f32[1,128]{1,0:T(1,128)} %bitcast.11, ...), custom_call_target="tpu_custom_call" | custom-call | flops 12000000000 | bytes 10485760 | tf_op jit(solution)/shard_map/pallas_call | solution.py:300
  59.5 4.0 %copy.13 = bf16[1,96,128,128]{3,2,1,0:T(8,128)(2,1)} copy(bf16[1,96,128,128]{3,2,1,0:T(8,128)(2,1)} %bitcast.6) | data formatting | bytes 6291456

commit v3 on v2

--- a/solution.py
+++ b/solution.py
@@ -26,10 +26,10 @@
 
 
 def kernel(
-    fact_hbm, own_v, cnt_v, cnt_s, nb_v, ent_hbm, gain_v, wself_hbm, wnbr_hbm, bias_v, wmid_hbm, wout_hbm,
+    fact_hbm, own_hbm, cnt_hbm, cnt1_hbm, nb_hbm, ent_hbm, gain_hbm, wself_hbm, wnbr_hbm, bias_hbm, wmid_hbm, wout_hbm,
     o_ref,
-    facts, ent, w1, wmid, wout, bs, bq, st, r1, r2, fin, nbs, rnb, wide, tab_v, nbt_v, tab_s, nb_s, mean_v, scale_v,
-    in1, send, xs, ags, ex, ea, lsem, s1, q1, s2, q2, s3, q3, sn, qn, sx, qx, sa, qa, ss, qs,
+    own_v, cnt_v, cnt_s, nb_v, gain_v, bias_v, facts, ent, w1, wmid, wout, bs, bq, st, r1, r2, fin, nbs, rnb, wide, tab_v, nbt_v, tab_s, nb_s, mean_v, scale_v,
+    in1, send, xs, ags, ex, ea, lsem, s1, q1, s2, q2, s3, q3, sn, qn, sx, qx, sa, qa, ss, qs, tsem,
 ):
     t = lax.axis_index("tm")
     s = lax.axis_index("hash")
@@ -39,6 +39,20 @@
         pl.semaphore_signal(bar, inc=1, device_id={"tm": lax.rem(t + i, TM)}, device_id_type=MESH)
     for d in range(1, HOLD):
         pl.semaphore_signal(bar, inc=1, device_id={"hash": peer(s, d // 4, d % 4)}, device_id_type=MESH)
+
+    def group(src, dst, n, send_sem, recv_sem):
+        return pltpu.make_async_remote_copy(
+            src_ref=src.at[pl.ds(0, n)], dst_ref=dst.at[pl.ds(0, n)], send_sem=send_sem.at[0],
+            recv_sem=recv_sem.at[0], device_id={"hash": peer(s, 0, 1)}, device_id_type=MESH,
+        )
+
+    first = group(st, r1, TM - 1, s1, q1)
+    asks = group(nbs, rnb, HOLD - 1, sn, qn)
+    second = group(r2, r2, HOLD - 1, s2, q2)
+    third = group(fin, fin, TM - 1, s3, q3)
+    early_x = group(xs, ex, HOLD - 1, sx, qx)
+    early_a = group(ags, ea, HOLD - 1, sa, qa)
+    rows_out = group(send, o_ref, (HOLD - 1) * (CAP - 1), ss, qs)
 
     per = B // CHUNKS
     loads = [
@@ -52,8 +66,18 @@
         pltpu.make_async_copy(wout_hbm, wout, lsem.at[CHUNKS + 3]),
         pltpu.make_async_copy(ent_hbm, ent, lsem.at[CHUNKS + 4]),
     ]
-    for cp in loads + rest:
+    tables = [
+        pltpu.make_async_copy(own_hbm, own_v, tsem.at[0]),
+        pltpu.make_async_copy(cnt_hbm, cnt_v, tsem.at[1]),
+        pltpu.make_async_copy(cnt1_hbm, cnt_s, tsem.at[2]),
+        pltpu.make_async_copy(nb_hbm, nb_v, tsem.at[3]),
+        pltpu.make_async_copy(gain_hbm, gain_v, tsem.at[4]),
+        pltpu.make_async_copy(bias_hbm, bias_v, tsem.at[5]),
+    ]
+    for cp in tables + loads + rest:
         cp.start()
+    for cp in tables:
+        cp.wait()
 
     hot = (lax.broadcasted_iota(jnp.int32, (HOLD, B), 0) == own_v[...]).astype(F32)
     upper = (
@@ -113,53 +137,35 @@
 
     pl.semaphore_wait(bar, TM - 1 + HOLD - 1)
 
-    first = []
     for i in range(1, TM):
         p = lax.rem(t + i, TM)
-        first.append(
-            pltpu.make_async_remote_copy(
-                src_ref=st.at[p], dst_ref=r1.at[t], send_sem=s1.at[i], recv_sem=q1.at[i],
+        pltpu.make_async_remote_copy(
+                src_ref=st.at[p], dst_ref=r1.at[t], send_sem=s1.at[0], recv_sem=q1.at[0],
                 device_id={"tm": p}, device_id_type=MESH,
-            )
-        )
-        first[-1].start()
-    asks = []
+        ).start()
     for d in range(1, HOLD):
         p = peer(s, d // 4, d % 4)
-        asks.append(
-            pltpu.make_async_remote_copy(
-                src_ref=nbs.at[p], dst_ref=rnb.at[s], send_sem=sn.at[d], recv_sem=qn.at[d],
+        pltpu.make_async_remote_copy(
+                src_ref=nbs.at[p], dst_ref=rnb.at[s], send_sem=sn.at[0], recv_sem=qn.at[0],
                 device_id={"hash": p}, device_id_type=MESH,
-            )
-        )
-        asks[-1].start()
-    early = []
+        ).start()
     for d in range(1, HOLD):
         p = peer(s, d // 4, d % 4)
-        early.append(
-            pltpu.make_async_remote_copy(
-                src_ref=xs.at[p], dst_ref=ex.at[s], send_sem=sx.at[d], recv_sem=qx.at[d],
+        pltpu.make_async_remote_copy(
+                src_ref=xs.at[p], dst_ref=ex.at[s], send_sem=sx.at[0], recv_sem=qx.at[0],
                 device_id={"hash": p}, device_id_type=MESH,
-            )
-        )
-        early[-1].start()
+        ).start()
     rnb[s] = nbs[s]
     r1[t] = st[t]
-    for cp in first:
-        cp.wait_recv()
+    first.wait_recv()
     r2[s] = jnp.sum(r1[...], axis=0)
-    second = []
     for d in range(1, HOLD):
         p = peer(s, d // 4, d % 4)
-        second.append(
-            pltpu.make_async_remote_copy(
-                src_ref=r2.at[s], dst_ref=r2.at[s], send_sem=s2.at[d], recv_sem=q2.at[d],
+        pltpu.make_async_remote_copy(
+                src_ref=r2.at[s], dst_ref=r2.at[s], send_sem=s2.at[0], recv_sem=q2.at[0],
                 device_id={"hash": p}, device_id_type=MESH,
-            )
-        )
-        second[-1].start()
-    for cp in asks:
-        cp.wait_recv()
+        ).start()
+    asks.wait_recv()
     for h in range(HOLD):
         nbt_v[h : h + 1, :] = rnb[h]
     nb_copy = pltpu.make_async_copy(nbt_v, nb_s, lsem.at[CHUNKS + 6])
@@ -176,30 +182,21 @@
         p = peer(s, d // 4, d % 4)
         if d:
             ags[p] = agg_of(p, CAP - 1)
-            early.append(
-                pltpu.make_async_remote_copy(
-                    src_ref=ags.at[p], dst_ref=ea.at[s], send_sem=sa.at[d], recv_sem=qa.at[d],
+            pltpu.make_async_remote_copy(
+                    src_ref=ags.at[p], dst_ref=ea.at[s], send_sem=sa.at[0], recv_sem=qa.at[0],
                     device_id={"hash": p}, device_id_type=MESH,
-                )
-            )
-            early[-1].start()
+            ).start()
         else:
             ea[s] = agg_of(p, CAP - 1)
-    for cp in second:
-        cp.wait_recv()
+    second.wait_recv()
     fin[t] = jnp.sum(r2[...], axis=0)
-    third = []
     for i in range(1, TM):
         p = lax.rem(t + i, TM)
-        third.append(
-            pltpu.make_async_remote_copy(
-                src_ref=fin.at[t], dst_ref=fin.at[t], send_sem=s3.at[i], recv_sem=q3.at[i],
+        pltpu.make_async_remote_copy(
+                src_ref=fin.at[t], dst_ref=fin.at[t], send_sem=s3.at[0], recv_sem=q3.at[0],
                 device_id={"tm": p}, device_id_type=MESH,
-            )
-        )
-        third[-1].start()
-    for cp in third:
-        cp.wait_recv()
+        ).start()
+    third.wait_recv()
     for h in range(HOLD):
         base = 3 * (h % 2)
         n = fin[h // 2, base + 2 : base + 3, :]
@@ -211,12 +208,12 @@
     def copy_of(dz, dx, c):
         k = (dz * 4 + dx) * CAP + c
         return pltpu.make_async_remote_copy(
-            src_ref=send.at[k], dst_ref=o_ref.at[s * CAP + c], send_sem=ss.at[k], recv_sem=qs.at[k],
+            src_ref=send.at[k], dst_ref=o_ref.at[s * CAP + c], send_sem=ss.at[0], recv_sem=qs.at[0],
             device_id={"hash": peer(s, dz, dx)}, device_id_type=MESH,
         )
 
     def own_copy(c):
-        return pltpu.make_async_copy(send.at[c], o_ref.at[s * CAP + c], ss.at[c])
+        return pltpu.make_async_copy(send.at[c], o_ref.at[s * CAP + c], lsem.at[CHUNKS + 7])
 
     def norm_of(x, p):
         x = (x.astype(F32) - mean_v[pl.ds(p, 1), :]) * scale_v[pl.ds(p, 1), :]
@@ -256,11 +253,11 @@
 
     lax.fori_loop(0, 4 * (CAP - 1), step, 0)
 
-    for cp in early:
-        cp.wait_recv()
+    early_x.wait_recv()
+    early_a.wait_recv()
 
     def late_copy(k):
-        return pltpu.make_async_copy(ea.at[k], o_ref.at[k * CAP + CAP - 1], ss.at[k * CAP + CAP - 1])
+        return pltpu.make_async_copy(ea.at[k], o_ref.at[k * CAP + CAP - 1], lsem.at[CHUNKS + 8])
 
     def late(n, carry):
         for i in range(4):
@@ -277,32 +274,28 @@
 
     lax.fori_loop(0, HOLD // 4, late, 0)
 
-    for cp in first + asks + second + third + early:
+    for cp in (first, asks, second, third, early_x, early_a, rows_out):
         cp.wait_send()
-    for c in range(CAP - 1):
-        own_copy(c).wait()
-    for k in range(HOLD):
-        late_copy(k).wait()
-
-    def finish(k, carry):
-        d, c = lax.div(k, CAP - 1) + 1, lax.rem(k, CAP - 1)
-        copy_of(lax.div(d, 4), lax.rem(d, 4), c).wait()
-        return carry
-
-    lax.fori_loop(0, (HOLD - 1) * (CAP - 1), finish, 0)
+    pltpu.make_async_copy(send.at[pl.ds(0, CAP - 1)], o_ref.at[pl.ds(0, CAP - 1)], lsem.at[CHUNKS + 7]).wait()
+    pltpu.make_async_copy(ea, o_ref.at[pl.ds(0, HOLD)], lsem.at[CHUNKS + 8]).wait()
+    rows_out.wait_recv()
 
 
 def body(fact_blocks, owners, row_counts, neighbours, entities, col_gain, w_self, w_nbr, mlp_bias, w_mid, w_out):
-    vmem = pl.BlockSpec(memory_space=pltpu.VMEM)
-    smem = pl.BlockSpec(memory_space=pltpu.SMEM)
     hbm = pl.BlockSpec(memory_space=pl.ANY)
     dma = pltpu.SemaphoreType.DMA
     out = pl.pallas_call(
         kernel,
         out_shape=jax.ShapeDtypeStruct((HOLD * CAP, R, D), BF16),
-        in_specs=[hbm, vmem, vmem, smem, vmem, hbm, vmem, hbm, hbm, vmem, hbm, hbm],
+        in_specs=[hbm] * 12,
         out_specs=hbm,
         scratch_shapes=[
+            pltpu.VMEM((1, B), jnp.int32),
+            pltpu.VMEM((1, B), jnp.int32),
+            pltpu.SMEM((B,), jnp.int32),
+            pltpu.VMEM((2 * CAP, 1, HOLD), jnp.int32),
+            pltpu.VMEM((1, D), F32),
+            pltpu.VMEM((1, HID), F32),
             pltpu.VMEM((B, R, D), BF16),
             pltpu.VMEM((64, R, D), BF16),
             pltpu.VMEM((2 * D, HID), BF16),
@@ -329,14 +322,9 @@
             pltpu.VMEM((HOLD, R, D), BF16),
             pltpu.VMEM((HOLD, R, D), BF16),
             pltpu.VMEM((HOLD, R, D), BF16),
-            dma((CHUNKS + 7,)),
-            dma((TM,)), dma((TM,)),
-            dma((HOLD,)), dma((HOLD,)),
-            dma((TM,)), dma((TM,)),
-            dma((HOLD,)), dma((HOLD,)),
-            dma((HOLD,)), dma((HOLD,)),
-            dma((HOLD,)), dma((HOLD,)),
-            dma((HOLD * CAP,)), dma((HOLD * CAP,)),
+            dma((CHUNKS + 9,)),
+            *[dma((1,))] * 14,
+            dma((6,)),
         ],
         compiler_params=pltpu.CompilerParams(
             collective_id=0, has_side_effects=True, vmem_limit_bytes=60 << 20

time: 63.6 us -> 59.5 us (0.936)
  Pallas kernels: 59.5 us -> 55.4 us
    pallas_call x1, Pallas kernels: 59.5 us -> 55.4 us  [body(): pl.pallas_call(kernel, out_shape=jax.ShapeDtypeStruct((HOLD * CAP, R, D),...]
where the time goes in v3:
time: 59.5 us; the launch traced here: 59.4 us
  Pallas kernels  55.4 us (93%)
  local copies, waits for them, and re-layouts  3.97 us (7%)
    pallas_call x1, Pallas kernels, body(): pl.pallas_call(kernel, out_shape=jax.ShapeDtypeStruct((HOLD * CAP, R, D),...  55.4 us
    unnamed x1, local copies, waits for them, and re-layouts  3.97 us

profile of v3, /device:TPU:1, one launch (start us, length us, event | category | flops | bytes accessed | tf_op | source)
XLA Modules:
  0.0 59.4 jit_solution(559470462367003483)
XLA Ops:
  0.0 55.4 %shard_map.109 = bf16[96,128,128]{2,1,0:T(8,128)(2,1)} custom-call(bf16[48,128,128]{2,1,0:T(8,128)(2,1)} %fact_hbm.1, s32[1,48]{1,0:T(1,128)} %bitcast.9, s32[1,48]{1,0:T(1,128)} %bitcast.10, s32[48]{0:T(128)} %cnt1_hbm.1, s32[12,1,16]{2,1,0:T(1,128)} %bitcast.7, bf16[64,128,128]{2,1,0:T(8,128)(2,1)} %ent_hbm.1, f32[1,128]{1,0:T(1,128)} %bitcast.11, ...), custom_call_target="tpu_custom_call" | custom-call | flops 12000000000 | bytes 10485760 | tf_op jit(solution)/shard_map/pallas_call | solution.py:287
  55.4 4.0 %copy.13 = bf16[1,96,128,128]{3,2,1,0:T(8,128)(2,1)} copy(bf16[1,96,128,128]{3,2,1,0:T(8,128)(2,1)} %bitcast.6) | data formatting | bytes 6291456

commit v4 on v3

--- a/solution.py
+++ b/solution.py
@@ -17,6 +17,7 @@
 HID = 512
 EPS = 1e-05
 CHUNKS = 4
+PIECES = 8
 F32 = jnp.float32
 BF16 = jnp.bfloat16
 
@@ -279,6 +280,21 @@
     pltpu.make_async_copy(send.at[pl.ds(0, CAP - 1)], o_ref.at[pl.ds(0, CAP - 1)], lsem.at[CHUNKS + 7]).wait()
     pltpu.make_async_copy(ea, o_ref.at[pl.ds(0, HOLD)], lsem.at[CHUNKS + 8]).wait()
     rows_out.wait_recv()
+
+
+def place(x_ref, o_ref, buf, rsem, wsem):
+    per = HOLD * CAP // PIECES
+    reads, writes = [], []
+    for k in range(PIECES):
+        part = pl.ds(k * per, per)
+        reads.append(pltpu.make_async_copy(x_ref.at[part], buf.at[part], rsem.at[k]))
+        writes.append(pltpu.make_async_copy(buf.at[part], o_ref.at[0, part], wsem.at[k]))
+        reads[-1].start()
+    for read, write in zip(reads, writes):
+        read.wait()
+        write.start()
+    for write in writes:
+        write.wait()
 
 
 def body(fact_blocks, owners, row_counts, neighbours, entities, col_gain, w_self, w_nbr, mlp_bias, w_mid, w_out):
@@ -344,7 +360,14 @@
         w_mid,
         w_out,
     )
-    return out[None]
+    return pl.pallas_call(
+        place,
+        out_shape=jax.ShapeDtypeStruct((1, HOLD * CAP, R, D), BF16),
+        in_specs=[hbm],
+        out_specs=hbm,
+        scratch_shapes=[pltpu.VMEM((HOLD * CAP, R, D), BF16), dma((PIECES,)), dma((PIECES,))],
+        compiler_params=pltpu.CompilerParams(vmem_limit_bytes=60 << 20),
+    )(out)
 
 
 def solution(mesh):

time: 59.5 us -> 58.3 us (0.980)
  local copies, waits for them, and re-layouts: 3.97 us -> 0 us
  Pallas kernels: 55.4 us -> 58.2 us
    unnamed x1 -> x0, local copies, waits for them, and re-layouts: 3.97 us -> none
    pallas_call x0 -> x1, Pallas kernels: none -> 2.79 us  [body(): pl.pallas_call(place, out_shape=jax.ShapeDtypeStruct((1, HOLD * CAP, R, D...]
where the time goes in v4:
time: 58.3 us; the launch traced here: 58.2 us
  Pallas kernels  58.2 us (100%)
    pallas_call x1, Pallas kernels, body(): pl.pallas_call(kernel, out_shape=jax.ShapeDtypeStruct((HOLD * CAP, R, D),...  55.4 us
    pallas_call x1, Pallas kernels, body(): pl.pallas_call(place, out_shape=jax.ShapeDtypeStruct((1, HOLD * CAP, R, D...  2.79 us

profile of v4, /device:TPU:1, one launch (start us, length us, event | category | flops | bytes accessed | tf_op | source)
XLA Modules:
  0.0 58.2 jit_solution(1140463645756782865)
XLA Ops:
  0.0 55.4 %shard_map.109.x_ref = bf16[96,128,128]{2,1,0:T(8,128)(2,1)} custom-call(bf16[48,128,128]{2,1,0:T(8,128)(2,1)} %fact_hbm.1, s32[1,48]{1,0:T(1,128)} %bitcast.7, s32[1,48]{1,0:T(1,128)} %bitcast.8, s32[48]{0:T(128)} %cnt1_hbm.1, s32[12,1,16]{2,1,0:T(1,128)} %bitcast.5, bf16[64,128,128]{2,1,0:T(8,128)(2,1)} %ent_hbm.1, f32[1,128]{1,0:T(1,128)} %bitcast.9, ...), custom_call_target="tpu_custom_call" | custom-call | flops 12000000000 | bytes 10485760 | tf_op jit(solution)/shard_map/pallas_call | solution.py:303
  55.4 2.8 %shard_map.110 = bf16[1,96,128,128]{3,2,1,0:T(8,128)(2,1)} custom-call(bf16[96,128,128]{2,1,0:T(8,128)(2,1)} %shard_map.109.x_ref), custom_call_target="tpu_custom_call" | custom-call | tf_op jit(solution)/shard_map/pallas_call | solution.py:363

commit v5 on v4

--- a/solution.py
+++ b/solution.py
@@ -35,11 +35,10 @@
     t = lax.axis_index("tm")
     s = lax.axis_index("hash")
 
-    bar = pltpu.get_barrier_semaphore()
-    for i in range(1, TM):
-        pl.semaphore_signal(bar, inc=1, device_id={"tm": lax.rem(t + i, TM)}, device_id_type=MESH)
-    for d in range(1, HOLD):
-        pl.semaphore_signal(bar, inc=1, device_id={"hash": peer(s, d // 4, d % 4)}, device_id_type=MESH)
+    zs = [lax.rem(lax.div(s, 4) + d, 4) * 4 for d in range(4)]
+    xc = [lax.rem(lax.rem(s, 4) + d, 4) for d in range(4)]
+    near = [s] + [zs[d // 4] + xc[d % 4] for d in range(1, HOLD)]
+    times = [t] + [lax.rem(t + i, TM) for i in range(1, TM)]
 
     def group(src, dst, n, send_sem, recv_sem):
         return pltpu.make_async_remote_copy(
@@ -75,7 +74,16 @@
         pltpu.make_async_copy(gain_hbm, gain_v, tsem.at[4]),
         pltpu.make_async_copy(bias_hbm, bias_v, tsem.at[5]),
     ]
-    for cp in tables + loads + rest:
+    for cp in tables + loads:
+        cp.start()
+
+    bar = pltpu.get_barrier_semaphore()
+    for i in range(1, TM):
+        pl.semaphore_signal(bar, inc=1, device_id={"tm": times[i]}, device_id_type=MESH)
+    for d in range(1, HOLD):
+        pl.semaphore_signal(bar, inc=1, device_id={"hash": near[d]}, device_id_type=MESH)
+
+    for cp in rest:
         cp.start()
     for cp in tables:
         cp.wait()
@@ -121,6 +129,7 @@
     squares = jnp.dot(hot, bq[...], preferred_element_type=F32, precision=lax.Precision.HIGHEST)
     live = jnp.broadcast_to(jnp.sum(hot * cnt, axis=1, keepdims=True), (HOLD, 128))
     st[...] = jnp.zeros_like(st)
+    fin[...] = jnp.zeros_like(fin)
     for h in range(HOLD):
         base = 3 * (h % 2)
         st[h // 2, base : base + 1, :] = sums[h : h + 1, :]
@@ -129,7 +138,7 @@
 
     tab_copy.wait()
     for d in range(HOLD):
-        p = peer(s, d // 4, d % 4)
+        p = near[d]
         x = facts[jnp.clip(tab_s[p, CAP - 1], 0, B - 1)]
         if d:
             xs[p] = x
@@ -139,38 +148,51 @@
     pl.semaphore_wait(bar, TM - 1 + HOLD - 1)
 
     for i in range(1, TM):
-        p = lax.rem(t + i, TM)
+        p = times[i]
         pltpu.make_async_remote_copy(
-                src_ref=st.at[p], dst_ref=r1.at[t], send_sem=s1.at[0], recv_sem=q1.at[0],
-                device_id={"tm": p}, device_id_type=MESH,
+            src_ref=st.at[p], dst_ref=r1.at[t], send_sem=s1.at[0], recv_sem=q1.at[0],
+            device_id={"tm": p}, device_id_type=MESH,
         ).start()
     for d in range(1, HOLD):
-        p = peer(s, d // 4, d % 4)
+        p = near[d]
         pltpu.make_async_remote_copy(
-                src_ref=nbs.at[p], dst_ref=rnb.at[s], send_sem=sn.at[0], recv_sem=qn.at[0],
-                device_id={"hash": p}, device_id_type=MESH,
+            src_ref=nbs.at[p], dst_ref=rnb.at[s], send_sem=sn.at[0], recv_sem=qn.at[0],
+            device_id={"hash": p}, device_id_type=MESH,
         ).start()
     for d in range(1, HOLD):
-        p = peer(s, d // 4, d % 4)
+        p = near[d]
         pltpu.make_async_remote_copy(
-                src_ref=xs.at[p], dst_ref=ex.at[s], send_sem=sx.at[0], recv_sem=qx.at[0],
-                device_id={"hash": p}, device_id_type=MESH,
+            src_ref=xs.at[p], dst_ref=ex.at[s], send_sem=sx.at[0], recv_sem=qx.at[0],
+            device_id={"hash": p}, device_id_type=MESH,
         ).start()
     rnb[s] = nbs[s]
     r1[t] = st[t]
     first.wait_recv()
     r2[s] = jnp.sum(r1[...], axis=0)
     for d in range(1, HOLD):
-        p = peer(s, d // 4, d % 4)
+        p = near[d]
         pltpu.make_async_remote_copy(
-                src_ref=r2.at[s], dst_ref=r2.at[s], send_sem=s2.at[0], recv_sem=q2.at[0],
-                device_id={"hash": p}, device_id_type=MESH,
+            src_ref=r2.at[s], dst_ref=r2.at[s], send_sem=s2.at[0], recv_sem=q2.at[0],
+            device_id={"hash": p}, device_id_type=MESH,
         ).start()
     asks.wait_recv()
     for h in range(HOLD):
         nbt_v[h : h + 1, :] = rnb[h]
     nb_copy = pltpu.make_async_copy(nbt_v, nb_s, lsem.at[CHUNKS + 6])
     nb_copy.start()
+    second.wait_recv()
+    total = jnp.sum(r2[...], axis=0)
+    for k in range(2):
+        mean = total[3 * k : 3 * k + 1, :] / total[3 * k + 2 : 3 * k + 3, :]
+        var = total[3 * k + 1 : 3 * k + 2, :] / total[3 * k + 2 : 3 * k + 3, :] - mean * mean
+        fin[t, 2 * k : 2 * k + 1, :] = mean
+        fin[t, 2 * k + 1 : 2 * k + 2, :] = lax.rsqrt(var + EPS) * gain_v[...]
+    for i in range(1, TM):
+        p = times[i]
+        pltpu.make_async_remote_copy(
+            src_ref=fin.at[t], dst_ref=fin.at[t], send_sem=s3.at[0], recv_sem=q3.at[0],
+            device_id={"tm": p}, device_id_type=MESH,
+        ).start()
     for cp in rest:
         cp.wait()
     nb_copy.wait()
@@ -180,7 +202,7 @@
         return (e * 0.5).astype(BF16)
 
     for d in range(HOLD):
-        p = peer(s, d // 4, d % 4)
+        p = near[d]
         if d:
             ags[p] = agg_of(p, CAP - 1)
             pltpu.make_async_remote_copy(
@@ -189,22 +211,10 @@
             ).start()
         else:
             ea[s] = agg_of(p, CAP - 1)
-    second.wait_recv()
-    fin[t] = jnp.sum(r2[...], axis=0)
-    for i in range(1, TM):
-        p = lax.rem(t + i, TM)
-        pltpu.make_async_remote_copy(
-                src_ref=fin.at[t], dst_ref=fin.at[t], send_sem=s3.at[0], recv_sem=q3.at[0],
-                device_id={"tm": p}, device_id_type=MESH,
-        ).start()
     third.wait_recv()
     for h in range(HOLD):
-        base = 3 * (h % 2)
-        n = fin[h // 2, base + 2 : base + 3, :]
-        mean = fin[h // 2, base : base + 1, :] / n
-        var = fin[h // 2, base + 1 : base + 2, :] / n - mean * mean
-        mean_v[h : h + 1, :] = mean
-        scale_v[h : h + 1, :] = lax.rsqrt(var + EPS) * gain_v[...]
+        mean_v[h : h + 1, :] = fin[h // 2, 2 * (h % 2) : 2 * (h % 2) + 1, :]
+        scale_v[h : h + 1, :] = fin[h // 2, 2 * (h % 2) + 1 : 2 * (h % 2) + 2, :]
 
     def copy_of(dz, dx, c):
         k = (dz * 4 + dx) * CAP + c

time: 58.3 us -> 58.1 us (level)
  no operation moved by 1% of the time
where the time goes in v5:
time: 58.1 us; the launch traced here: 58 us
  Pallas kernels  58 us (100%)
    pallas_call x1, Pallas kernels, body(): pl.pallas_call(kernel, out_shape=jax.ShapeDtypeStruct((HOLD * CAP, R, D),...  55.2 us
    pallas_call x1, Pallas kernels, body(): pl.pallas_call(place, out_shape=jax.ShapeDtypeStruct((1, HOLD * CAP, R, D...  2.79 us

profile of v5, /device:TPU:1, one launch (start us, length us, event | category | flops | bytes accessed | tf_op | source)
XLA Modules:
  0.0 58.0 jit_solution(1411719244881095777)
XLA Ops:
  0.0 55.2 %shard_map.109.x_ref = bf16[96,128,128]{2,1,0:T(8,128)(2,1)} custom-call(bf16[48,128,128]{2,1,0:T(8,128)(2,1)} %fact_hbm.1, s32[1,48]{1,0:T(1,128)} %bitcast.7, s32[1,48]{1,0:T(1,128)} %bitcast.8, s32[48]{0:T(128)} %cnt1_hbm.1, s32[12,1,16]{2,1,0:T(1,128)} %bitcast.5, bf16[64,128,128]{2,1,0:T(8,128)(2,1)} %ent_hbm.1, f32[1,128]{1,0:T(1,128)} %bitcast.9, ...), custom_call_target="tpu_custom_call" | custom-call | flops 12000000000 | bytes 10485760 | tf_op jit(solution)/shard_map/pallas_call | solution.py:313
  55.2 2.8 %shard_map.110 = bf16[1,96,128,128]{3,2,1,0:T(8,128)(2,1)} custom-call(bf16[96,128,128]{2,1,0:T(8,128)(2,1)} %shard_map.109.x_ref), custom_call_target="tpu_custom_call" | custom-call | tf_op jit(solution)/shard_map/pallas_call | solution.py:373

commit v6 on v5

--- a/solution.py
+++ b/solution.py
@@ -37,7 +37,7 @@
 
     zs = [lax.rem(lax.div(s, 4) + d, 4) * 4 for d in range(4)]
     xc = [lax.rem(lax.rem(s, 4) + d, 4) for d in range(4)]
-    near = [s] + [zs[d // 4] + xc[d % 4] for d in range(1, HOLD)]
+    near = [s] + [zs[d // 4] + xc[d % 4] for d in (10, 6, 9, 14, 11, 2, 8, 5, 7, 13, 15, 1, 4, 3, 12)]
     times = [t] + [lax.rem(t + i, TM) for i in range(1, TM)]
 
     def group(src, dst, n, send_sem, recv_sem):

time: 58.1 us -> 57.6 us (level)
  no operation moved by 1% of the time
where the time goes in v6:
time: 57.6 us; the launch traced here: 57.5 us
  Pallas kernels  57.5 us (100%)
    pallas_call x1, Pallas kernels, body(): pl.pallas_call(kernel, out_shape=jax.ShapeDtypeStruct((HOLD * CAP, R, D),...  54.7 us
    pallas_call x1, Pallas kernels, body(): pl.pallas_call(place, out_shape=jax.ShapeDtypeStruct((1, HOLD * CAP, R, D...  2.79 us

profile of v6, /device:TPU:1, one launch (start us, length us, event | category | flops | bytes accessed | tf_op | source)
XLA Modules:
  0.0 57.5 jit_solution(13983252829432019584)
XLA Ops:
  0.0 54.7 %shard_map.109.x_ref = bf16[96,128,128]{2,1,0:T(8,128)(2,1)} custom-call(bf16[48,128,128]{2,1,0:T(8,128)(2,1)} %fact_hbm.1, s32[1,48]{1,0:T(1,128)} %bitcast.7, s32[1,48]{1,0:T(1,128)} %bitcast.8, s32[48]{0:T(128)} %cnt1_hbm.1, s32[12,1,16]{2,1,0:T(1,128)} %bitcast.5, bf16[64,128,128]{2,1,0:T(8,128)(2,1)} %ent_hbm.1, f32[1,128]{1,0:T(1,128)} %bitcast.9, ...), custom_call_target="tpu_custom_call" | custom-call | flops 12000000000 | bytes 10485760 | tf_op jit(solution)/shard_map/pallas_call | solution.py:313
  54.7 2.8 %shard_map.110 = bf16[1,96,128,128]{3,2,1,0:T(8,128)(2,1)} custom-call(bf16[96,128,128]{2,1,0:T(8,128)(2,1)} %shard_map.109.x_ref), custom_call_target="tpu_custom_call" | custom-call | tf_op jit(solution)/shard_map/pallas_call | solution.py:373

commit v7 on v6

--- a/solution.py
+++ b/solution.py
@@ -238,7 +238,7 @@
         return jnp.dot(h2, wout[...], preferred_element_type=F32)
 
     def step(n, carry):
-        c, dz = lax.div(n, 4), lax.rem(n, 4)
+        c, dz = lax.div(n, 4), lax.rem(n + 2, 4)
         for dx in range(4):
             p = peer(s, dz, dx)
             in1[dx * R : (dx + 1) * R, 0:D] = norm_of(facts[jnp.clip(tab_s[p, c], 0, B - 1)], p)

time: 57.6 us -> 57.4 us (level)
  no operation moved by 1% of the time
where the time goes in v7:
time: 57.4 us; the launch traced here: 57.3 us
  Pallas kernels  57.3 us (100%)
    pallas_call x1, Pallas kernels, body(): pl.pallas_call(kernel, out_shape=jax.ShapeDtypeStruct((HOLD * CAP, R, D),...  54.5 us
    pallas_call x1, Pallas kernels, body(): pl.pallas_call(place, out_shape=jax.ShapeDtypeStruct((1, HOLD * CAP, R, D...  2.79 us

profile of v7, /device:TPU:1, one launch (start us, length us, event | category | flops | bytes accessed | tf_op | source)
XLA Modules:
  0.0 57.3 jit_solution(2910248114798930087)
XLA Ops:
  0.0 54.5 %shard_map.109.x_ref = bf16[96,128,128]{2,1,0:T(8,128)(2,1)} custom-call(bf16[48,128,128]{2,1,0:T(8,128)(2,1)} %fact_hbm.1, s32[1,48]{1,0:T(1,128)} %bitcast.7, s32[1,48]{1,0:T(1,128)} %bitcast.8, s32[48]{0:T(128)} %cnt1_hbm.1, s32[12,1,16]{2,1,0:T(1,128)} %bitcast.5, bf16[64,128,128]{2,1,0:T(8,128)(2,1)} %ent_hbm.1, f32[1,128]{1,0:T(1,128)} %bitcast.9, ...), custom_call_target="tpu_custom_call" | custom-call | flops 12000000000 | bytes 10485760 | tf_op jit(solution)/shard_map/pallas_call | solution.py:313
  54.5 2.8 %shard_map.110 = bf16[1,96,128,128]{3,2,1,0:T(8,128)(2,1)} custom-call(bf16[96,128,128]{2,1,0:T(8,128)(2,1)} %shard_map.109.x_ref), custom_call_target="tpu_custom_call" | custom-call | tf_op jit(solution)/shard_map/pallas_call | solution.py:373

commit v8 on v6

--- a/solution.py
+++ b/solution.py
@@ -216,10 +216,11 @@
         mean_v[h : h + 1, :] = fin[h // 2, 2 * (h % 2) : 2 * (h % 2) + 1, :]
         scale_v[h : h + 1, :] = fin[h // 2, 2 * (h % 2) + 1 : 2 * (h % 2) + 2, :]
 
-    def copy_of(dz, dx, c):
+    def copy_of(dz, dx, c, half):
         k = (dz * 4 + dx) * CAP + c
         return pltpu.make_async_remote_copy(
-            src_ref=send.at[k], dst_ref=o_ref.at[s * CAP + c], send_sem=ss.at[0], recv_sem=qs.at[0],
+            src_ref=send.at[k, pl.ds(half * (R // 2), R // 2)],
+            dst_ref=o_ref.at[s * CAP + c, pl.ds(half * (R // 2), R // 2)], send_sem=ss.at[0], recv_sem=qs.at[0],
             device_id={"hash": peer(s, dz, dx)}, device_id_type=MESH,
         )
 
@@ -249,12 +250,14 @@
             y = jnp.where(row < tab_s[p, 16 + c], out[dx * R : (dx + 1) * R, :], 0.0)
             send[(dz * 4 + dx) * CAP + c] = y.astype(BF16)
             if dx:
-                copy_of(dz, dx, c).start()
+                for half in range(2):
+                    copy_of(dz, dx, c, half).start()
             else:
 
                 @pl.when(dz > 0)
                 def _():
-                    copy_of(dz, 0, c).start()
+                    for half in range(2):
+                        copy_of(dz, 0, c, half).start()
 
                 @pl.when(dz == 0)
                 def _():

time: 57.6 us -> 57.6 us (level)
  no operation moved by 1% of the time
where the time goes in v8:
time: 57.6 us; the launch traced here: 57.5 us
  Pallas kernels  57.5 us (100%)
    pallas_call x1, Pallas kernels, body(): pl.pallas_call(kernel, out_shape=jax.ShapeDtypeStruct((HOLD * CAP, R, D),...  54.7 us
    pallas_call x1, Pallas kernels, body(): pl.pallas_call(place, out_shape=jax.ShapeDtypeStruct((1, HOLD * CAP, R, D...  2.79 us

profile of v8, /device:TPU:1, one launch (start us, length us, event | category | flops | bytes accessed | tf_op | source)
XLA Modules:
  0.0 57.5 jit_solution(18102192315726416996)
XLA Ops:
  0.0 54.7 %shard_map.109.x_ref = bf16[96,128,128]{2,1,0:T(8,128)(2,1)} custom-call(bf16[48,128,128]{2,1,0:T(8,128)(2,1)} %fact_hbm.1, s32[1,48]{1,0:T(1,128)} %bitcast.7, s32[1,48]{1,0:T(1,128)} %bitcast.8, s32[48]{0:T(128)} %cnt1_hbm.1, s32[12,1,16]{2,1,0:T(1,128)} %bitcast.5, bf16[64,128,128]{2,1,0:T(8,128)(2,1)} %ent_hbm.1, f32[1,128]{1,0:T(1,128)} %bitcast.9, ...), custom_call_target="tpu_custom_call" | custom-call | flops 12000000000 | bytes 10485760 | tf_op jit(solution)/shard_map/pallas_call | solution.py:316
  54.7 2.8 %shard_map.110 = bf16[1,96,128,128]{3,2,1,0:T(8,128)(2,1)} custom-call(bf16[96,128,128]{2,1,0:T(8,128)(2,1)} %shard_map.109.x_ref), custom_call_target="tpu_custom_call" | custom-call | tf_op jit(solution)/shard_map/pallas_call | solution.py:376
